TPU v7x, 32 devices: a whole 2x2x4 slice. The times are simulated.
32 devices in a mesh: row: 8 (over y, x, core), col: 4 (over z).
Axes of the slice: x: 2, y: 2, z: 4, core: 2. Of those that a mesh axis runs over, the one named last changes fastest.
Arguments:
- counts: int32 [4096, 4096], P('row', 'col'), may hold values from 1 to 5
- sample_weights: float32 [4096, 4096], P('row', 'col'), may hold values from 0.045 to 54
- classes: int32 [4096, 4096], P('row', 'col'), may hold values from 0 to 3
- class_radius: int32 [4], replicated, may hold values from 8 to 64, as said below
Outputs:
- density_first: float32 [4096, 4096], P('row', 'col')
- density_second: float32 [4096, 4096], P('row', 'col')
Inputs may be any that keep to these rules, and one draw needn't show every extreme that they name: `class_radius`: the radii rise strictly from class 0 to class 3, and class 3's radius is 64.
All inputs are finite; a program needn't handle non-finite values.
Results may differ from a plain program's by a relative error of at most 0.0001.
Values sent between devices are 32-bit elements; how exact they have to be, the bound alone decides.
A program may use at most 128 MiB of HBM per device.

v0:
```python
import jax
import jax.numpy as jnp
from jax import lax
from jax.sharding import PartitionSpec as P

RMAX = 64
PR = 32


BACKGROUND = 0.5
HIGHEST_PRECISION = lax.Precision.HIGHEST


def with_halo(block, sides, width):
    for axis, dim in sides:
        count = lax.axis_size(axis)
        forward = [(i, i + 1) for i in range(count - 1)]
        backward = [(target, source) for source, target in forward]
        low = lax.ppermute(
            lax.slice_in_dim(block, block.shape[dim] - width, None, axis=dim), axis, forward
        )
        high = lax.ppermute(lax.slice_in_dim(block, 0, width, axis=dim), axis, backward)
        block = jnp.concatenate([low, block, high], axis=dim)
    return block


def band_pair(radius, reach):
    spread = 0.5 * radius
    offsets = jnp.arange(-reach, reach + 1).astype(jnp.float32)
    inside = (jnp.abs(offsets) <= radius).astype(jnp.float32)
    norm_sum = jnp.sum(jnp.exp(-offsets * offsets / (2.0 * spread * spread)) * inside)
    source = jnp.arange(4 * reach)[:, None]
    target = jnp.arange(2 * reach)[None, :]
    shifts = (source - target - reach).astype(jnp.float32)
    weight = (
        jnp.exp(-shifts * shifts / (2.0 * spread * spread))
        * (jnp.abs(shifts) <= radius).astype(jnp.float32)
        / norm_sum
    )
    return (weight[: 2 * reach], weight[2 * reach :])


def columns_one(field, band_upper, band_lower):
    block_width = band_upper.shape[0]
    blocks = field.reshape(field.shape[0], field.shape[1] // block_width, block_width)
    result = jnp.einsum("mjk,ko->mjo", blocks[:, :-1], band_upper, precision=HIGHEST_PRECISION)
    result = result + jnp.einsum(
        "mjk,ko->mjo", blocks[:, 1:], band_lower, precision=HIGHEST_PRECISION
    )
    return result.reshape(field.shape[0], -1)


def rows_one(field, band_upper, band_lower):
    block_width = band_upper.shape[0]
    blocks = field.reshape(field.shape[0] // block_width, block_width, field.shape[1])
    result = jnp.einsum("jkn,ko->jon", blocks[:-1], band_upper, precision=HIGHEST_PRECISION)
    result = result + jnp.einsum("jkn,ko->jon", blocks[1:], band_lower, precision=HIGHEST_PRECISION)
    return result.reshape(-1, field.shape[1])


def rows_every(field, band_upper, band_lower):
    block_width = band_upper.shape[1]
    blocks = field.reshape(
        field.shape[0], field.shape[1] // block_width, block_width, field.shape[2]
    )
    result = jnp.einsum("cjkn,cko->cjon", blocks[:, :-1], band_upper, precision=HIGHEST_PRECISION)
    result = result + jnp.einsum(
        "cjkn,cko->cjon", blocks[:, 1:], band_lower, precision=HIGHEST_PRECISION
    )
    return result.reshape(field.shape[0], -1, field.shape[2])


def columns_summed(field, band_upper, band_lower):
    block_width = band_upper.shape[1]
    blocks = field.reshape(
        field.shape[0], field.shape[1], field.shape[2] // block_width, block_width
    )
    result = jnp.einsum("cmjk,cko->mjo", blocks[:, :, :-1], band_upper, precision=HIGHEST_PRECISION)
    result = result + jnp.einsum(
        "cmjk,cko->mjo", blocks[:, :, 1:], band_lower, precision=HIGHEST_PRECISION
    )
    return result.reshape(field.shape[1], -1)


def first_sweep(padded, class_rim, band_upper, band_lower, every_fn):
    labels = jnp.arange(band_upper.shape[0])[:, None, None]
    stacked = jnp.where(class_rim[None] == labels, padded[None], jnp.float32(0.0))
    return every_fn(stacked, band_upper, band_lower)


def spread_classes(adapted, class_rim, band_upper, band_lower):
    padded = with_halo(adapted, (("row", 0),), RMAX)
    swept = first_sweep(padded, class_rim, band_upper, band_lower, rows_every)
    widened = with_halo(swept, (("col", 2),), RMAX)
    return columns_summed(widened, band_upper, band_lower)


def body(counts, sample_weights, classes, class_radius):
    cell_mass = counts.astype(jnp.float32) * sample_weights
    pilot_upper, pilot_lower = band_pair(jnp.float32(PR), PR)
    band_upper, band_lower = jax.vmap(lambda radius: band_pair(radius, RMAX))(
        class_radius.astype(jnp.float32)
    )
    padded = with_halo(cell_mass, (("col", 1),), PR)
    smoothed = columns_one(padded, pilot_upper, pilot_lower)
    padded = with_halo(smoothed, (("row", 0),), PR)
    pilot_field = rows_one(padded, pilot_upper, pilot_lower) + BACKGROUND
    class_rim = with_halo(classes, (("row", 0),), RMAX)
    mass_sum = lax.psum(jnp.sum(cell_mass), ("row", "col"))
    results = []
    for iteration in range(2):
        log_terms = jnp.sum(cell_mass * jnp.log(pilot_field))
        mean_log = lax.psum(log_terms, ("row", "col")) / mass_sum
        adapted = cell_mass * pilot_field / jnp.exp(mean_log)
        density = spread_classes(adapted, class_rim, band_upper, band_lower)
        results.append(density)
        pilot_field = density + BACKGROUND
    return (results[0], results[1])


def solution(mesh):
    return jax.shard_map(
        body,
        mesh=mesh,
        in_specs=(P("row", "col"), P("row", "col"), P("row", "col"), P()),
        out_specs=(P("row", "col"), P("row", "col")),
        check_vma=False,
    )
```

profile of v0, /device:TPU:5, one launch (start us, length us, event | category | flops | bytes accessed | tf_op | source)
XLA Modules:
  0.0 340.2 jit_solution(8413940075368686357)
XLA Ops:
  32.1 4.6 %collective-permute-start.5 = (f32[32,1024]{0,1:T(8,128)S(1)}, f32[32,1024]{0,1:T(8,128)S(1)}, u32[]{:S(2)}, u32[]{:S(2)}) collective-permute-start(f32[32,1024]{0,1:T(8,128)S(1)} %bitcast.106), channel_id=1, source_target_pairs={{4,0},{8,4},{12,8},{16,12},{20,16},{24,20},{28,24},{5,1},{9,5},{13... | collective-permute-start | bytes 393224 | tf_op jit(solution)/shard_map/ppermute | solution.py:22
  39.2 4.7 %collective-permute-done.5 = f32[32,1024]{0,1:T(8,128)S(1)} collective-permute-done((f32[32,1024]{0,1:T(8,128)S(1)}, f32[32,1024]{0,1:T(8,128)S(1)}, u32[]{:S(2)}, u32[]{:S(2)}) %collective-permute-start.5) | collective-permute-done | bytes 131104 | tf_op jit(solution)/shard_map/ppermute | solution.py:22
  43.9 4.8 %collective-permute-done.4 = f32[32,1024]{0,1:T(8,128)S(1)} collective-permute-done((f32[32,1024]{0,1:T(8,128)S(1)}, f32[32,1024]{0,1:T(8,128)S(1)}, u32[]{:S(2)}, u32[]{:S(2)}) %collective-permute-start.4) | collective-permute-done | bytes 131104 | tf_op jit(solution)/shard_map/ppermute | solution.py:19
  65.9 42.5 %all-reduce = (f32[]{:T(128)}, f32[]{:T(128)}) all-reduce(f32[]{:T(128)} %get-tuple-element.9, f32[]{:T(128)} %get-tuple-element.8), channel_id=1, replica_groups=mesh['row'=8,'col'=4] {'row','col'}, use_global_device_ids=true, to_apply=%region_3.0 | all-reduce | flops 2 | bytes 16 | tf_op jit(solution)/shard_map/psum | solution.py:113
  112.1 4.5 %collective-permute-start.6 = (f32[64,1024]{1,0:T(8,128)S(1)}, f32[64,1024]{1,0:T(8,128)S(1)}, u32[]{:S(2)}, u32[]{:S(2)}) collective-permute-start(f32[64,1024]{1,0:T(8,128)S(1)} %get-tuple-element.20), channel_id=1, source_target_pairs={{0,4},{4,8},{8,12},{12,16},{16,20},{20,24},{24,28},{1,5},{5,9},{9,... | collective-permute-start | bytes 786440 | tf_op jit(solution)/shard_map/ppermute | solution.py:19
  119.8 4.4 %collective-permute-done.7 = f32[64,1024]{1,0:T(8,128)S(1)} collective-permute-done((f32[64,1024]{1,0:T(8,128)S(1)}, f32[64,1024]{1,0:T(8,128)S(1)}, u32[]{:S(2)}, u32[]{:S(2)}) %collective-permute-start.7) | collective-permute-done | bytes 262176 | tf_op jit(solution)/shard_map/ppermute | solution.py:22
  129.3 9.5 %fusion.6 = f32[4,128,4,1024]{3,1,2,0:T(8,128)} fusion(f32[4,5,128,1024]{3,2,1,0:T(8,128)S(1)} %fusion.1, f32[4,256,128]{1,2,0:T(8,128)S(1)} %fusion.20), kind=kOutput, calls=%fused_computation.9 | convolution fusion | flops 3221225472 | bytes 17039360 | tf_op jit(solution)/shard_map/cjkn,cko->cjon/dot_general | solution.py:67
  138.8 11.7 %fusion.10 = f32[4,128,4,1024]{3,1,2,0:T(8,128)} fusion(f32[4,128,4,1024]{3,1,2,0:T(8,128)} %fusion.6, f32[4,5,128,1024]{3,2,1,0:T(8,128)S(1)} %fusion.1, f32[4,256,128]{1,2,0:T(8,128)S(1)} %fusion.20), kind=kOutput, calls=%fused_computation.13 | convolution fusion | flops 3223322624 | bytes 25427968 | tf_op jit(solution)/shard_map/cjkn,cko->cjon/dot_general | solution.py:66
  150.5 8.7 %copy.31 = f32[4,512,1024]{1,2,0:T(8,128)} copy(f32[4,512,1024]{2,1,0:T(8,128)} %bitcast.92) | data formatting | bytes 16777216 | tf_op jit(solution)/shard_map/reshape | solution.py:70
  165.2 10.1 %collective-permute-done.8 = f32[4,512,64]{1,2,0:T(8,128)S(1)} collective-permute-done((f32[4,512,64]{1,2,0:T(8,128)S(1)}, f32[4,512,64]{1,2,0:T(8,128)S(1)}, u32[]{:S(2)}, u32[]{:S(2)}) %collective-permute-start.8) | collective-permute-done | bytes 524320 | tf_op jit(solution)/shard_map/ppermute | solution.py:19
  179.4 8.3 %pad_maximum_fusion = f32[4,512,1152]{1,2,0:T(8,128)} fusion(f32[4,512,64]{1,2,0:T(8,128)} %collective-permute-done.9, f32[4,512,1024]{1,2,0:T(8,128)} %copy.31, f32[4,512,64]{1,2,0:T(8,128)S(1)} %collective-permute-done.8), kind=kLoop, calls=%fused_computation.3 | loop fusion | flops 4718592 | bytes 18874368 | tf_op jit(solution)/shard_map/concatenate | solution.py:23
  187.8 7.6 %fusion.22 = f32[512,8,128,1]{0,2,1,3:T(8,128)S(1)} fusion(f32[4,512,9,128]{1,3,2,0:T(8,128)} %bitcast.90, f32[4,256,128]{1,2,0:T(8,128)S(1)} %fusion.20), kind=kOutput, calls=%fused_computation.39 | convolution fusion | flops 3221225472 | bytes 11796480 | tf_op jit(solution)/shard_map/cmjk,cko->mjo/dot_general | solution.py:78
  195.4 6.4 %bitcast_add_fusion.1 = f32[512,8,128]{0,2,1:T(8,128)} fusion(f32[512,8,128,1]{0,2,1,3:T(8,128)S(1)} %fusion.22, f32[4,512,9,128]{1,3,2,0:T(8,128)S(1)} %bitcast.91, f32[4,256,128]{1,2,0:T(8,128)S(1)} %fusion.20), kind=kOutput, calls=%fused_computation.21 | convolution fusion | flops 3221749760 | bytes 13893632 | tf_op jit(solution)/shard_map/cmjk,cko->mjo/dot_general | solution.py:79
  207.5 39.4 %psum.23 = f32[]{:T(128)} all-reduce(f32[]{:T(128)} %multiply_reduce_fusion), channel_id=1, replica_groups=mesh['row'=8,'col'=4] {'row','col'}, use_global_device_ids=true, to_apply=%region_7.8 | all-reduce | flops 1 | bytes 8 | tf_op jit(solution)/shard_map/psum | solution.py:113
  250.4 4.5 %collective-permute-start.10 = (f32[64,1024]{1,0:T(8,128)S(1)}, f32[64,1024]{1,0:T(8,128)S(1)}, u32[]{:S(2)}, u32[]{:S(2)}) collective-permute-start(f32[64,1024]{1,0:T(8,128)S(1)} %get-tuple-element.16), channel_id=1, source_target_pairs={{0,4},{4,8},{8,12},{12,16},{16,20},{20,24},{24,28},{1,5},{5,9},{9,... | collective-permute-start | bytes 786440 | tf_op jit(solution)/shard_map/ppermute | solution.py:19
  258.1 4.7 %collective-permute-done.11 = f32[64,1024]{1,0:T(8,128)S(1)} collective-permute-done((f32[64,1024]{1,0:T(8,128)S(1)}, f32[64,1024]{1,0:T(8,128)S(1)}, u32[]{:S(2)}, u32[]{:S(2)}) %collective-permute-start.11) | collective-permute-done | bytes 262176 | tf_op jit(solution)/shard_map/ppermute | solution.py:22
  267.9 9.5 %fusion.2 = f32[4,128,4,1024]{3,1,2,0:T(8,128)} fusion(f32[4,5,128,1024]{3,2,1,0:T(8,128)S(1)} %fusion, f32[4,256,128]{1,2,0:T(8,128)S(1)} %fusion.20), kind=kOutput, calls=%fused_computation.5 | convolution fusion | flops 3221225472 | bytes 17039360 | tf_op jit(solution)/shard_map/cjkn,cko->cjon/dot_general | solution.py:67
  277.4 11.7 %fusion.13 = f32[4,128,4,1024]{3,1,2,0:T(8,128)} fusion(f32[4,128,4,1024]{3,1,2,0:T(8,128)} %fusion.2, f32[4,5,128,1024]{3,2,1,0:T(8,128)S(1)} %fusion, f32[4,256,128]{1,2,0:T(8,128)S(1)} %fusion.20), kind=kOutput, calls=%fused_computation.14 | convolution fusion | flops 3223322624 | bytes 25427968 | tf_op jit(solution)/shard_map/cjkn,cko->cjon/dot_general | solution.py:66
  289.1 8.7 %copy.37 = f32[4,512,1024]{1,2,0:T(8,128)} copy(f32[4,512,1024]{2,1,0:T(8,128)} %bitcast.93) | data formatting | bytes 16777216 | tf_op jit(solution)/shard_map/reshape | solution.py:70
  303.0 9.7 %collective-permute-done.12 = f32[4,512,64]{1,2,0:T(8,128)S(1)} collective-permute-done((f32[4,512,64]{1,2,0:T(8,128)S(1)}, f32[4,512,64]{1,2,0:T(8,128)S(1)}, u32[]{:S(2)}, u32[]{:S(2)}) %collective-permute-start.12) | collective-permute-done | bytes 524320 | tf_op jit(solution)/shard_map/ppermute | solution.py:19
  312.7 4.3 %collective-permute-done.13 = f32[4,512,64]{1,2,0:T(8,128)S(1)} collective-permute-done((f32[4,512,64]{1,2,0:T(8,128)S(1)}, f32[4,512,64]{1,2,0:T(8,128)S(1)}, u32[]{:S(2)}, u32[]{:S(2)}) %collective-permute-start.13) | collective-permute-done | bytes 524320 | tf_op jit(solution)/shard_map/ppermute | solution.py:22
  317.0 8.2 %pad_maximum_fusion.1 = f32[4,512,1152]{1,2,0:T(8,128)} fusion(f32[4,512,64]{1,2,0:T(8,128)S(1)} %collective-permute-done.13, f32[4,512,1024]{1,2,0:T(8,128)} %copy.37, f32[4,512,64]{1,2,0:T(8,128)S(1)} %collective-permute-done.12), kind=kLoop, calls=%fused_computation.4 | loop fusion | flops 4718592 | bytes 18874368 | tf_op jit(solution)/shard_map/concatenate | solution.py:23
  325.2 7.6 %fusion.21 = f32[512,8,128,1]{0,2,1,3:T(8,128)S(1)} fusion(f32[4,512,9,128]{1,3,2,0:T(8,128)} %bitcast.88, f32[4,256,128]{1,2,0:T(8,128)S(1)} %fusion.20), kind=kOutput, calls=%fused_computation.38 | convolution fusion | flops 3221225472 | bytes 11796480 | tf_op jit(solution)/shard_map/cmjk,cko->mjo/dot_general | solution.py:78
  332.8 5.1 %bitcast_add_fusion = f32[512,8,128]{0,2,1:T(8,128)S(1)} fusion(f32[512,8,128,1]{0,2,1,3:T(8,128)S(1)} %fusion.21, f32[4,512,9,128]{1,3,2,0:T(8,128)S(1)} %bitcast.89, f32[4,256,128]{1,2,0:T(8,128)S(1)} %fusion.20), kind=kOutput, calls=%fused_computation.20 | convolution fusion | flops 3221749760 | bytes 13893632 | tf_op jit(solution)/shard_map/cmjk,cko->mjo/dot_general | solution.py:79
  (72 shorter events, 94.7 us)
Async XLA Ops:
  2.5 116.7 %collective-permute-start = (s32[64,1024]{1,0:T(8,128)}, s32[64,1024]{1,0:T(8,128)S(1)}, u32[]{:S(2)}, u32[]{:S(2)}) collective-permute-start(s32[64,1024]{1,0:T(8,128)} %get-tuple-element.18), channel_id=1, source_target_pairs={{0,4},{4,8},{8,12},{12,16},{16,20},{20,24},{24,28},{1,5},{5,9},{9,... | collective-permute-start | bytes 786440 | tf_op jit(solution)/shard_map/ppermute | solution.py:19
  6.2 10.9 %copy-start.8 = (s32[4]{0:T(128)S(1)}, s32[4]{0:T(128)}, u32[]{:S(2)}) copy-start(s32[4]{0:T(128)} %param.7) | copy-start | bytes 52
  6.2 113.0 %collective-permute-start.1 = (s32[64,1024]{1,0:T(8,128)}, s32[64,1024]{1,0:T(8,128)S(1)}, u32[]{:S(2)}, u32[]{:S(2)}) collective-permute-start(s32[64,1024]{1,0:T(8,128)} %get-tuple-element.19), channel_id=1, source_target_pairs={{4,0},{8,4},{12,8},{16,12},{20,16},{24,20},{28,24},{5,1},{9,5},{13... | collective-permute-start | bytes 786440 | tf_op jit(solution)/shard_map/ppermute | solution.py:22
  11.1 8.2 %collective-permute-start.3 = (f32[512,32]{1,0:T(8,128)S(1)}, f32[512,32]{1,0:T(8,128)S(1)}, u32[]{:S(2)}, u32[]{:S(2)}) collective-permute-start(f32[512,32]{1,0:T(8,128)S(1)} %get-tuple-element.26), channel_id=1, source_target_pairs={{1,0},{2,1},{3,2},{5,4},{6,5},{7,6},{9,8},{10,9},{11,10},{13,12},{... | collective-permute-start | bytes 196616 | tf_op jit(solution)/shard_map/ppermute | solution.py:22
  12.4 7.8 %collective-permute-start.2 = (f32[512,32]{1,0:T(8,128)S(1)}, f32[512,32]{1,0:T(8,128)S(1)}, u32[]{:S(2)}, u32[]{:S(2)}) collective-permute-start(f32[512,32]{1,0:T(8,128)S(1)} %get-tuple-element.27), channel_id=1, source_target_pairs={{0,1},{1,2},{2,3},{4,5},{5,6},{6,7},{8,9},{9,10},{10,11},{12,13},{... | collective-permute-start | bytes 196616 | tf_op jit(solution)/shard_map/ppermute | solution.py:19
  25.8 3.8 %copy-start.4 = (f32[512,1088]{0,1:T(8,128)S(1)}, f32[512,1088]{0,1:T(8,128)}, u32[]{:S(2)}) copy-start(f32[512,1088]{0,1:T(8,128)} %copy.28) | copy-start | bytes 6684676
  32.1 11.8 %collective-permute-start.5 = (f32[32,1024]{0,1:T(8,128)S(1)}, f32[32,1024]{0,1:T(8,128)S(1)}, u32[]{:S(2)}, u32[]{:S(2)}) collective-permute-start(f32[32,1024]{0,1:T(8,128)S(1)} %bitcast.106), channel_id=1, source_target_pairs={{4,0},{8,4},{12,8},{16,12},{20,16},{24,20},{28,24},{5,1},{9,5},{13... | collective-permute-start | bytes 393224 | tf_op jit(solution)/shard_map/ppermute | solution.py:22
  36.7 11.9 %collective-permute-start.4 = (f32[32,1024]{0,1:T(8,128)S(1)}, f32[32,1024]{0,1:T(8,128)S(1)}, u32[]{:S(2)}, u32[]{:S(2)}) collective-permute-start(f32[32,1024]{0,1:T(8,128)S(1)} %bitcast.105), channel_id=1, source_target_pairs={{0,4},{4,8},{8,12},{12,16},{16,20},{20,24},{24,28},{1,5},{5,9},{9,... | collective-permute-start | bytes 393224 | tf_op jit(solution)/shard_map/ppermute | solution.py:19
  57.7 3.6 %copy-start.6 = (f32[512,1024]{1,0:T(8,128)S(1)}, f32[512,1024]{1,0:T(8,128)}, u32[]{:S(2)}) copy-start(f32[512,1024]{1,0:T(8,128)} %copy.29) | copy-start | bytes 6291460
  63.4 1.3 copy-start.5
  109.8 9.4 %copy-start.7 = (s32[512,1024]{1,0:T(8,128)S(1)}, s32[512,1024]{1,0:T(8,128)}, u32[]{:S(2)}) copy-start(s32[512,1024]{1,0:T(8,128)} %param.6) | copy-start | bytes 6291460
  112.1 7.8 %collective-permute-start.6 = (f32[64,1024]{1,0:T(8,128)S(1)}, f32[64,1024]{1,0:T(8,128)S(1)}, u32[]{:S(2)}, u32[]{:S(2)}) collective-permute-start(f32[64,1024]{1,0:T(8,128)S(1)} %get-tuple-element.20), channel_id=1, source_target_pairs={{0,4},{4,8},{8,12},{12,16},{16,20},{20,24},{24,28},{1,5},{5,9},{9,... | collective-permute-start | bytes 786440 | tf_op jit(solution)/shard_map/ppermute | solution.py:19
  116.5 7.7 %collective-permute-start.7 = (f32[64,1024]{1,0:T(8,128)S(1)}, f32[64,1024]{1,0:T(8,128)S(1)}, u32[]{:S(2)}, u32[]{:S(2)}) collective-permute-start(f32[64,1024]{1,0:T(8,128)S(1)} %get-tuple-element.21), channel_id=1, source_target_pairs={{4,0},{8,4},{12,8},{16,12},{20,16},{24,20},{28,24},{5,1},{9,5},{13... | collective-permute-start | bytes 786440 | tf_op jit(solution)/shard_map/ppermute | solution.py:22
  119.5 6.4 %copy-start.2 = (s32[640,1024]{1,0:T(8,128)}, s32[640,1024]{1,0:T(8,128)S(1)}, u32[]{:S(2)}) copy-start(s32[640,1024]{1,0:T(8,128)S(1)} %pad_add_fusion) | copy-start | bytes 7864324
  160.5 14.9 %collective-permute-start.8 = (f32[4,512,64]{1,2,0:T(8,128)S(1)}, f32[4,512,64]{1,2,0:T(8,128)S(1)}, u32[]{:S(2)}, u32[]{:S(2)}) collective-permute-start(f32[4,512,64]{1,2,0:T(8,128)S(1)} %get-tuple-element.14), channel_id=1, source_target_pairs={{0,1},{1,2},{2,3},{4,5},{5,6},{6,7},{8,9},{9,10},{10,11},{12,13},{... | collective-permute-start | bytes 1572872 | tf_op jit(solution)/shard_map/ppermute | solution.py:19
  163.8 15.7 %collective-permute-start.9 = (f32[4,512,64]{1,2,0:T(8,128)S(1)}, f32[4,512,64]{1,2,0:T(8,128)}, u32[]{:S(2)}, u32[]{:S(2)}) collective-permute-start(f32[4,512,64]{1,2,0:T(8,128)S(1)} %get-tuple-element.15), channel_id=1, source_target_pairs={{1,0},{2,1},{3,2},{5,4},{6,5},{7,6},{9,8},{10,9},{11,10},{13,12},{... | collective-permute-start | bytes 1572872 | tf_op jit(solution)/shard_map/ppermute | solution.py:22
  187.8 7.6 %copy-start.1 = (f32[4,512,1152]{1,2,0:T(8,128)S(1)}, f32[4,512,1152]{1,2,0:T(8,128)}, u32[]{:S(2)}) copy-start(f32[4,512,1152]{1,2,0:T(8,128)} %pad_maximum_fusion) | copy-start | bytes 28311556
  250.4 7.8 %collective-permute-start.10 = (f32[64,1024]{1,0:T(8,128)S(1)}, f32[64,1024]{1,0:T(8,128)S(1)}, u32[]{:S(2)}, u32[]{:S(2)}) collective-permute-start(f32[64,1024]{1,0:T(8,128)S(1)} %get-tuple-element.16), channel_id=1, source_target_pairs={{0,4},{4,8},{8,12},{12,16},{16,20},{20,24},{24,28},{1,5},{5,9},{9,... | collective-permute-start | bytes 786440 | tf_op jit(solution)/shard_map/ppermute | solution.py:19
  254.9 9.6 %copy-start.3 = (s32[640,1024]{1,0:T(8,128)S(1)}, s32[640,1024]{1,0:T(8,128)}, u32[]{:S(2)}) copy-start(s32[640,1024]{1,0:T(8,128)} %copy-done.2) | copy-start | bytes 7864324
  254.9 8.0 %collective-permute-start.11 = (f32[64,1024]{1,0:T(8,128)S(1)}, f32[64,1024]{1,0:T(8,128)S(1)}, u32[]{:S(2)}, u32[]{:S(2)}) collective-permute-start(f32[64,1024]{1,0:T(8,128)S(1)} %get-tuple-element.17), channel_id=1, source_target_pairs={{4,0},{8,4},{12,8},{16,12},{20,16},{24,20},{28,24},{5,1},{9,5},{13... | collective-permute-start | bytes 786440 | tf_op jit(solution)/shard_map/ppermute | solution.py:22
  299.1 13.7 %collective-permute-start.12 = (f32[4,512,64]{1,2,0:T(8,128)S(1)}, f32[4,512,64]{1,2,0:T(8,128)S(1)}, u32[]{:S(2)}, u32[]{:S(2)}) collective-permute-start(f32[4,512,64]{1,2,0:T(8,128)S(1)} %get-tuple-element.12), channel_id=1, source_target_pairs={{0,1},{1,2},{2,3},{4,5},{5,6},{6,7},{8,9},{9,10},{10,11},{12,13},{... | collective-permute-start | bytes 1572872 | tf_op jit(solution)/shard_map/ppermute | solution.py:19
  301.4 15.6 %collective-permute-start.13 = (f32[4,512,64]{1,2,0:T(8,128)S(1)}, f32[4,512,64]{1,2,0:T(8,128)S(1)}, u32[]{:S(2)}, u32[]{:S(2)}) collective-permute-start(f32[4,512,64]{1,2,0:T(8,128)S(1)} %get-tuple-element.13), channel_id=1, source_target_pairs={{1,0},{2,1},{3,2},{5,4},{6,5},{7,6},{9,8},{10,9},{11,10},{13,12},{... | collective-permute-start | bytes 1572872 | tf_op jit(solution)/shard_map/ppermute | solution.py:22
  325.2 7.6 %copy-start = (f32[4,512,1152]{1,2,0:T(8,128)S(1)}, f32[4,512,1152]{1,2,0:T(8,128)}, u32[]{:S(2)}) copy-start(f32[4,512,1152]{1,2,0:T(8,128)} %pad_maximum_fusion.1) | copy-start | bytes 28311556
where the time goes:
time: 346 us; the launch traced here: 340 us
  blocking collectives  81.9 us (24%)
  matrix products  80.9 us (23%)
  waiting for transfers between devices  50.4 us (15%)
  other arithmetic  42.9 us (12%)
  starting transfers between devices  40.2 us (12%)
  local copies, waits for them, and re-layouts  39.6 us (11%)
  between operations  4.23 us (1%)
    psum x2, blocking collectives, body(): mean_log = lax.psum(log_terms, ('row', 'col')) / mass_sum  81.9 us
    ppermute x7, waiting for transfers between devices, with_halo(): lax.ppermute(lax.slice_in_dim(block, block.shape[dim] - width, None, axis...  26.7 us
    ppermute x7, starting transfers between devices, with_halo(): lax.ppermute(lax.slice_in_dim(block, block.shape[dim] - width, None, axis...  24.5 us
    ppermute x7, waiting for transfers between devices, with_halo(): lax.ppermute(lax.slice_in_dim(block, 0, width, axis=dim), axis, backward)  23.7 us
    concatenate x6, other arithmetic, with_halo(): block = jnp.concatenate([low, block, high], axis=dim)  23.5 us
    dot_general x2, matrix products, rows_every(): jnp.einsum('cjkn,cko->cjon', blocks[:, :-1], band_upper, precision=HIGHES...  23.4 us
    dot_general x2, matrix products, rows_every(): jnp.einsum('cjkn,cko->cjon', blocks[:, 1:], band_lower, precision=HIGHEST...  19 us
    reshape x2, local copies, waits for them, and re-layouts, rows_every(): return result.reshape(field.shape[0], -1, field.shape[2])  17.4 us
  transfers between devices with their start and end apart: 14, of which 12 were waited for; matrix products, arithmetic and copies ran while one was open for 10% of the time, Pallas kernels for 0%

commit v1 on v0

v1 whole, which is shorter than its diff:
```python
import functools

import jax
import jax.numpy as jnp
from jax import lax
from jax.experimental import pallas as pl
from jax.experimental.pallas import tpu as pltpu
from jax.sharding import PartitionSpec as P

RMAX = 64
PR = 32
BACKGROUND = 0.5
B = 2 * RMAX
K = 2 * B
CHUNK = 16
MESH = pl.DeviceIdType.MESH
F32 = jnp.float32
BF16 = jnp.bfloat16


def split(x):
    high = x.astype(BF16)
    return high, (x - high.astype(F32)).astype(BF16)


def dot(a, b):
    return jnp.dot(a, b, preferred_element_type=F32)


def band(radius, source_dim):
    shape = (K, B) if source_dim == 0 else (B, K)
    source = lax.broadcasted_iota(jnp.int32, shape, source_dim)
    target = lax.broadcasted_iota(jnp.int32, shape, 1 - source_dim)
    spread = 0.5 * radius
    factor = 1.0 / (2.0 * spread * spread)

    def raw(d):
        return jnp.where(jnp.abs(d) <= radius, jnp.exp(-d * d * factor), 0.0)

    offsets = lax.broadcasted_iota(jnp.int32, (8, K), 1) - B
    norm = jnp.sum(raw(offsets.astype(F32))[0:1], axis=1, keepdims=True)
    return raw((source - target - RMAX).astype(F32)) / norm


def kernel(
    rows, cols, classes_n,
    radius_ref, counts_ref, weights_ref, classes_ref,
    first_ref, second_ref,
    mass, field, padded, high, low, mask, swept_h, swept_l,
    row_band, col_band, halo_top, halo_bottom, halo_left, halo_right, corner,
    part, red_row, red_col,
    send_sem, recv_sem, rsend, rrecv, csend, crecv,
):
    r, c = lax.axis_index("row"), lax.axis_index("col")
    tr, tc = counts_ref.shape
    wide = tc + 2 * RMAX
    last = wide - B
    chunks = tr // CHUNK

    steps = [(-1, 0), (1, 0), (0, -1), (0, 1), (-1, -1), (-1, 1), (1, -1), (1, 1)]

    def there(dr, dc):
        ok = jnp.bool_(True)
        if dr < 0:
            ok = ok & (r > 0)
        if dr > 0:
            ok = ok & (r < rows - 1)
        if dc < 0:
            ok = ok & (c > 0)
        if dc > 0:
            ok = ok & (c < cols - 1)
        return ok

    barrier = pltpu.get_barrier_semaphore()
    for d in range(1, rows):
        pl.semaphore_signal(barrier, 1, device_id=(lax.rem(r + d, rows), c), device_id_type=MESH)
    for d in range(1, cols):
        pl.semaphore_signal(barrier, 1, device_id=(r, lax.rem(c + d, cols)), device_id_type=MESH)
    for dr, dc in steps[4:]:
        @pl.when(there(dr, dc))
        def _():
            pl.semaphore_signal(barrier, 1, device_id=(r + dr, c + dc), device_id_type=MESH)
    vertical = (r > 0).astype(jnp.int32) + (r < rows - 1).astype(jnp.int32)
    across = (c > 0).astype(jnp.int32) + (c < cols - 1).astype(jnp.int32)
    pl.semaphore_wait(barrier, rows + cols - 2 + vertical * across)

    def pieces(phase):
        own = padded.at[phase]
        top, bottom = pl.ds(0, RMAX), pl.ds(tr - RMAX, RMAX)
        left, right = pl.ds(0, B), pl.ds(last, B)
        return [
            (own.at[top, :], halo_bottom.at[phase], 1),
            (own.at[bottom, :], halo_top.at[phase], 0),
            (own.at[:, left], halo_right.at[phase], 3),
            (own.at[:, right], halo_left.at[phase], 2),
            (own.at[top, left], corner.at[phase, 3], 7),
            (own.at[top, right], corner.at[phase, 2], 6),
            (own.at[bottom, left], corner.at[phase, 1], 5),
            (own.at[bottom, right], corner.at[phase, 0], 4),
        ]

    def copy_of(phase, n):
        dr, dc = steps[n]
        source, target, slot = pieces(phase)[n]
        return pltpu.make_async_remote_copy(
            src_ref=source, dst_ref=target,
            send_sem=send_sem.at[phase, n], recv_sem=recv_sem.at[phase, slot],
            device_id=(r + dr, c + dc), device_id_type=MESH,
        )

    landing = lambda phase: [
        halo_top.at[phase], halo_bottom.at[phase], halo_left.at[phase], halo_right.at[phase],
        corner.at[phase, 0], corner.at[phase, 1], corner.at[phase, 2], corner.at[phase, 3],
    ]

    def send(phase):
        for n in range(8):
            dr, dc = steps[n]

            @pl.when(there(dr, dc))
            def _():
                copy_of(phase, n).start()

    def clear(phase):
        for n in range(8):
            dr, dc = steps[n]

            @pl.when(jnp.logical_not(there(dr, dc)))
            def _():
                ref = landing(phase)[n]
                ref[...] = jnp.zeros(ref.shape, F32)

    def arrived(phase, which):
        for n in which:
            dr, dc = steps[n]

            @pl.when(there(dr, dc))
            def _():
                ref = landing(phase)[n]
                pltpu.make_async_remote_copy(
                    src_ref=ref, dst_ref=ref, send_sem=send_sem.at[phase, n],
                    recv_sem=recv_sem.at[phase, n],
                    device_id=(r + dr, c + dc), device_id_type=MESH,
                ).wait_recv()

    def sent(phase):
        for n in range(8):
            dr, dc = steps[n]

            @pl.when(there(dr, dc))
            def _():
                copy_of(phase, n).wait_send()

    def shifted(x):
        full = jnp.concatenate([x, jnp.zeros((x.shape[0], 2 * RMAX), F32)], axis=1)
        return pltpu.roll(full, RMAX, axis=1)

    def tile_sum(x):
        total = None
        for a in range(0, x.shape[0], 8):
            for b in range(0, x.shape[1], 128):
                piece = x[a : a + 8, b : b + 128]
                total = piece if total is None else total + piece
        return total

    CLS, PIL, ONE, TWO = 0, 1, 2, 3

    def prepare(i, total):
        at = pl.ds(pl.multiple_of(i * CHUNK, CHUNK), CHUNK)
        inner = pl.ds(pl.multiple_of(i * CHUNK + RMAX, CHUNK), CHUNK)
        m = counts_ref[at, :].astype(F32) * weights_ref[at, :]
        mass[at, :] = m
        s = shifted(m)
        padded[PIL, at, :] = s
        high[inner, :], low[inner, :] = split(s)
        return total + tile_sum(m)

    mass_total = lax.fori_loop(0, chunks, prepare, jnp.zeros((8, 128), F32))
    send(PIL)

    def labels(i, _):
        at = pl.ds(pl.multiple_of(i * CHUNK, CHUNK), CHUNK)
        padded[CLS, at, :] = shifted((classes_ref[at, :] + 1).astype(F32))
        return 0

    lax.fori_loop(0, chunks, labels, 0)
    send(CLS)
    for phase in range(4):
        clear(phase)

    for n in range(classes_n + 1):
        radius = F32(PR) if n == classes_n else radius_ref[n].astype(F32)
        h, l = split(band(radius, 1))
        row_band[n, 0:B, :] = h
        row_band[n, B : 2 * B, :] = l
        h, l = split(band(radius, 0))
        both = jnp.concatenate([h, l], axis=1)
        col_band[n, 0:K, :] = both
        col_band[n, K : 2 * K, :] = both

    def put(at, across, x, masks):
        if masks:
            for n in range(classes_n):
                mask[n, at, across] = jnp.where(x == n + 1.0, 1.0, 0.0).astype(BF16)
        else:
            high[at, across], low[at, across] = split(x)

    inside = pl.ds(B, last - B)

    def rows_in(phase, masks=False):
        def step(i, _):
            at = pl.ds(pl.multiple_of(i * CHUNK, CHUNK), CHUNK)
            below = pl.ds(pl.multiple_of(i * CHUNK + RMAX + tr, CHUNK), CHUNK)
            put(at, inside, halo_top[phase, at, inside], masks)
            put(below, inside, halo_bottom[phase, at, inside], masks)
            return 0

        lax.fori_loop(0, RMAX // CHUNK, step, 0)

    def cols_in(phase, masks=False):
        left, right = pl.ds(0, B), pl.ds(last, B)

        def step(i, _):
            at = pl.ds(pl.multiple_of(i * CHUNK, CHUNK), CHUNK)
            below = pl.ds(pl.multiple_of(i * CHUNK + RMAX + tr, CHUNK), CHUNK)
            put(at, left, halo_top[phase, at, left] + corner[phase, 0, at, :], masks)
            put(at, right, halo_top[phase, at, right] + corner[phase, 1, at, :], masks)
            put(below, left, halo_bottom[phase, at, left] + corner[phase, 2, at, :], masks)
            put(below, right, halo_bottom[phase, at, right] + corner[phase, 3, at, :], masks)
            return 0

        lax.fori_loop(0, RMAX // CHUNK, step, 0)

        def middle(i, _):
            at = pl.ds(pl.multiple_of(i * CHUNK, CHUNK), CHUNK)
            inner = pl.ds(pl.multiple_of(i * CHUNK + RMAX, CHUNK), CHUNK)
            put(inner, left, padded[phase, at, left] + halo_left[phase, at, :], masks)
            put(inner, right, padded[phase, at, right] + halo_right[phase, at, :], masks)
            return 0

        lax.fori_loop(0, chunks, middle, 0)

    def row_piece(i, places, labelled):
        source = pl.ds(pl.multiple_of(i * B, B), K)
        target = pl.ds(pl.multiple_of(i * B, B), B)

        def get(ref, *lead):
            got = [ref[(*lead, source, pl.ds(start, size))] for start, size in places]
            return got[0] if len(got) == 1 else jnp.concatenate(got, axis=1)

        h, l = get(high), get(low)
        for n in range(classes_n) if labelled else (0,):
            if labelled:
                m = get(mask, n)
                xh, xl = h * m, l * m
            else:
                xh, xl = h, l
            w = row_band[n if labelled else classes_n]
            main = dot(w, xh)
            y = main[:B] + main[B:] + dot(w[:B], xl)
            yh, yl = split(y)
            offset = 0
            for start, size in places:
                swept_h[n, target, pl.ds(start, size)] = yh[:, offset : offset + size]
                swept_l[n, target, pl.ds(start, size)] = yl[:, offset : offset + size]
                offset += size

    blocks = tr // B
    pairs = (last - B) // (2 * B)
    odd = (last - B) % (2 * B)

    def row_blocks(indices, labelled):
        low_i, count, stride = indices

        def step(s, _):
            i = low_i + s * stride

            def inner(q, _):
                row_piece(i, [(pl.multiple_of(B + q * 2 * B, B), 2 * B)], labelled)
                return 0

            lax.fori_loop(0, pairs, inner, 0)
            if odd:
                row_piece(i, [(last - odd, odd)], labelled)
            return 0

        lax.fori_loop(0, count, step, 0)

    def edge_blocks(labelled):
        def step(i, _):
            row_piece(i, [(0, B), (last, B)], labelled)
            return 0

        lax.fori_loop(0, blocks, step, 0)

    def col_sweep(target, labelled):
        def step(j, _):
            window = pl.ds(pl.multiple_of(j * B, B), K)
            total = None
            for n in range(classes_n) if labelled else (0,):
                x = jnp.concatenate([swept_h[n, :, window], swept_l[n, :, window]], axis=1)
                term = dot(x, col_band[n if labelled else classes_n])
                total = term if total is None else total + term
            target[:, pl.ds(pl.multiple_of(j * B, B), B)] = total[:, :B] + total[:, B:]
            return 0

        lax.fori_loop(0, tc // B, step, 0)

    def sweep(phase, labelled, between=()):
        between = list(between) + [lambda: None] * 2
        row_blocks((1, blocks - 2, 1), labelled)
        between[0]()
        arrived(phase, (0, 1))
        rows_in(phase)
        row_blocks((0, 2, blocks - 1), labelled)
        between[1]()
        arrived(phase, range(2, 8))
        cols_in(phase)
        edge_blocks(labelled)

    def row_copy(t, d):
        return pltpu.make_async_remote_copy(
            src_ref=part.at[t, 0], dst_ref=red_row.at[t, d],
            send_sem=rsend.at[t, d], recv_sem=rrecv.at[t, d],
            device_id=(lax.rem(r + d, rows), c), device_id_type=MESH,
        )

    def col_copy(t, d):
        return pltpu.make_async_remote_copy(
            src_ref=part.at[t, 1], dst_ref=red_col.at[t, d],
            send_sem=csend.at[t, d], recv_sem=crecv.at[t, d],
            device_id=(r, lax.rem(c + d, cols)), device_id_type=MESH,
        )

    def reduce_start(t, log_total):
        part[t, 0, 0:8, :] = mass_total
        part[t, 0, 8:16, :] = log_total
        for d in range(1, rows):
            row_copy(t, d).start()

    def reduce_middle(t):
        total = part[t, 0]
        for d in range(1, rows):
            row_copy(t, d).wait()
            total = total + red_row[t, d]
        part[t, 1] = total
        for d in range(1, cols):
            col_copy(t, d).start()

    def reduce_end(t):
        total = part[t, 1]
        for d in range(1, cols):
            col_copy(t, d).wait()
            total = total + red_col[t, d]
        mass_sum = jnp.sum(total[0:8], keepdims=True)
        log_sum = jnp.sum(total[8:16], keepdims=True)
        return jnp.exp(-(log_sum / mass_sum))

    def adapt(phase, density_of):
        def step(i, total):
            at = pl.ds(pl.multiple_of(i * CHUNK, CHUNK), CHUNK)
            inner = pl.ds(pl.multiple_of(i * CHUNK + RMAX, CHUNK), CHUNK)
            pilot = density_of(at) + BACKGROUND
            m = mass[at, :]
            s = shifted(m * pilot)
            padded[phase, at, :] = s
            high[inner, :], low[inner, :] = split(s)
            return total + tile_sum(m * jnp.log(pilot))

        total = lax.fori_loop(0, chunks, step, jnp.zeros((8, 128), F32))
        send(phase)
        return total

    sweep(PIL, False)
    col_sweep(field, False)
    log_total = adapt(ONE, lambda at: field[at, :])
    reduce_start(0, log_total)

    def own_masks(i, _):
        at = pl.ds(pl.multiple_of(i * CHUNK, CHUNK), CHUNK)
        inner = pl.ds(pl.multiple_of(i * CHUNK + RMAX, CHUNK), CHUNK)
        put(inner, inside, padded[CLS, at, inside], True)
        return 0

    lax.fori_loop(0, chunks, own_masks, 0)
    arrived(CLS, range(8))
    rows_in(CLS, True)
    cols_in(CLS, True)

    sweep(ONE, True, [lambda: reduce_middle(0)])
    col_sweep(field, True)
    inverse = reduce_end(0)

    def first_density(at):
        density = field[at, :] * inverse
        first_ref[at, :] = density
        return density

    log_total = adapt(TWO, first_density)
    reduce_start(1, log_total)

    sweep(TWO, True, [lambda: reduce_middle(1)])
    col_sweep(field, True)
    inverse_two = reduce_end(1)

    def finish(i, _):
        at = pl.ds(pl.multiple_of(i * CHUNK, CHUNK), CHUNK)
        second_ref[at, :] = field[at, :] * inverse_two
        return 0

    lax.fori_loop(0, chunks, finish, 0)
    for phase in range(4):
        sent(phase)


def body(rows, cols, counts, sample_weights, classes, class_radius):
    tr, tc = counts.shape
    n = class_radius.shape[0]
    wide, tall = tc + 2 * RMAX, tr + 2 * RMAX
    vmem = pl.BlockSpec(memory_space=pltpu.VMEM)
    out = jax.ShapeDtypeStruct((tr, tc), F32)
    return pl.pallas_call(
        functools.partial(kernel, rows, cols, n),
        out_shape=(out, out),
        in_specs=[pl.BlockSpec(memory_space=pltpu.SMEM), vmem, vmem, vmem],
        out_specs=(vmem, vmem),
        scratch_shapes=[
            pltpu.VMEM((tr, tc), F32),
            pltpu.VMEM((tr, tc), F32),
            pltpu.VMEM((4, tr, wide), F32),
            pltpu.VMEM((tall, wide), BF16),
            pltpu.VMEM((tall, wide), BF16),
            pltpu.VMEM((n, tall, wide), BF16),
            pltpu.VMEM((n, tr, wide), BF16),
            pltpu.VMEM((n, tr, wide), BF16),
            pltpu.VMEM((n + 1, 2 * B, K), BF16),
            pltpu.VMEM((n + 1, 2 * K, 2 * B), BF16),
            pltpu.VMEM((4, RMAX, wide), F32),
            pltpu.VMEM((4, RMAX, wide), F32),
            pltpu.VMEM((4, tr, B), F32),
            pltpu.VMEM((4, tr, B), F32),
            pltpu.VMEM((4, 4, RMAX, B), F32),
            pltpu.VMEM((2, 2, 16, 128), F32),
            pltpu.VMEM((2, rows, 16, 128), F32),
            pltpu.VMEM((2, cols, 16, 128), F32),
            pltpu.SemaphoreType.DMA((4, 8)),
            pltpu.SemaphoreType.DMA((4, 8)),
            pltpu.SemaphoreType.DMA((2, rows)),
            pltpu.SemaphoreType.DMA((2, rows)),
            pltpu.SemaphoreType.DMA((2, cols)),
            pltpu.SemaphoreType.DMA((2, cols)),
        ],
        compiler_params=pltpu.CompilerParams(
            collective_id=0, has_side_effects=True, vmem_limit_bytes=60 * 2**20
        ),
    )(class_radius, counts, sample_weights, classes)


def solution(mesh):
    rows, cols = mesh.shape["row"], mesh.shape["col"]
    return jax.shard_map(
        functools.partial(body, rows, cols),
        mesh=mesh,
        in_specs=(P("row", "col"), P("row", "col"), P("row", "col"), P()),
        out_specs=(P("row", "col"), P("row", "col")),
        check_vma=False,
    )
```

time: 346 us -> 81.3 us (0.23)
  the two profiles are of different devices: /device:TPU:5 before, /device:TPU:12 now
where the time goes in v1:
time: 81.3 us; the launch traced here: 80.6 us
  Pallas kernels  75.3 us (93%)
  local copies, waits for them, and re-layouts  4.63 us (6%)
    pallas_call x1, Pallas kernels, body(): pl.pallas_call(functools.partial(kernel, rows, cols, n), out_shape=(out,...  75.3 us
    unnamed x4, local copies, waits for them, and re-layouts  4.63 us

profile of v1, /device:TPU:12, one launch (start us, length us, event | category | flops | bytes accessed | tf_op | source)
XLA Modules:
  0.0 80.6 jit_solution(3447480144047059286)
XLA Ops:
  0.6 75.3 %shard_map.59 = (f32[512,1024]{1,0:T(8,128)}, f32[512,1024]{1,0:T(8,128)}) custom-call(s32[4]{0:T(128)} %radius_ref.1, s32[512,1024]{1,0:T(8,128)} %counts_ref.1, f32[512,1024]{1,0:T(8,128)} %weights_ref.1, s32[512,1024]{1,0:T(8,128)} %classes_ref.1), custom_call_target="tpu_custom_call" | custom-call | tf_op jit(solution)/shard_map/pallas_call | solution.py:422
  76.0 0.0 copy-start
  76.0 3.3 %copy.8 = f32[512,1024]{1,0:T(8,128)} copy(f32[512,1024]{1,0:T(8,128)} %get-tuple-element.4) | data formatting | bytes 4194304
  79.3 0.0 copy-done
  79.3 1.3 %copy.9 = f32[512,1024]{1,0:T(8,128)} copy(f32[512,1024]{1,0:T(8,128)S(1)} %copy-done) | data formatting | bytes 4194304
Async XLA Ops:
  76.0 3.3 %copy-start = (f32[512,1024]{1,0:T(8,128)S(1)}, f32[512,1024]{1,0:T(8,128)}, u32[]{:S(2)}) copy-start(f32[512,1024]{1,0:T(8,128)} %get-tuple-element.5) | copy-start | bytes 6291460

commit v2 on v1

--- a/solution.py
+++ b/solution.py
@@ -12,8 +12,9 @@
 BACKGROUND = 0.5
 B = 2 * RMAX
 K = 2 * B
-CHUNK = 16
+CHUNK = 64
 MESH = pl.DeviceIdType.MESH
+CLS, PIL, ONE, TWO = 0, 1, 2, 3
 F32 = jnp.float32
 BF16 = jnp.bfloat16
 
@@ -45,8 +46,8 @@
 def kernel(
     rows, cols, classes_n,
     radius_ref, counts_ref, weights_ref, classes_ref,
-    first_ref, second_ref,
-    mass, field, padded, high, low, mask, swept_h, swept_l,
+    first_ref, second_ref, inverse_ref,
+    mass, field, padded, packed, high, low, mask, swept_h, swept_l,
     row_band, col_band, halo_top, halo_bottom, halo_left, halo_right, corner,
     part, red_row, red_col,
     send_sem, recv_sem, rsend, rrecv, csend, crecv,
@@ -86,17 +87,19 @@
 
     def pieces(phase):
         own = padded.at[phase]
-        top, bottom = pl.ds(0, RMAX), pl.ds(tr - RMAX, RMAX)
+        reach = PR if phase == PIL else RMAX
+        top, bottom = pl.ds(0, reach), pl.ds(tr - reach, reach)
+        far, near = pl.ds(RMAX - reach, reach), pl.ds(0, reach)
         left, right = pl.ds(0, B), pl.ds(last, B)
         return [
-            (own.at[top, :], halo_bottom.at[phase], 1),
-            (own.at[bottom, :], halo_top.at[phase], 0),
-            (own.at[:, left], halo_right.at[phase], 3),
-            (own.at[:, right], halo_left.at[phase], 2),
-            (own.at[top, left], corner.at[phase, 3], 7),
-            (own.at[top, right], corner.at[phase, 2], 6),
-            (own.at[bottom, left], corner.at[phase, 1], 5),
-            (own.at[bottom, right], corner.at[phase, 0], 4),
+            (own.at[top, :], halo_bottom.at[phase, near], 1),
+            (own.at[bottom, :], halo_top.at[phase, far], 0),
+            (packed.at[phase, 0], halo_right.at[phase], 3),
+            (packed.at[phase, 1], halo_left.at[phase], 2),
+            (own.at[top, left], corner.at[phase, 3, near], 7),
+            (own.at[top, right], corner.at[phase, 2, near], 6),
+            (own.at[bottom, left], corner.at[phase, 1, far], 5),
+            (own.at[bottom, right], corner.at[phase, 0, far], 4),
         ]
 
     def copy_of(phase, n):
@@ -108,12 +111,29 @@
             device_id=(r + dr, c + dc), device_id_type=MESH,
         )
 
-    landing = lambda phase: [
-        halo_top.at[phase], halo_bottom.at[phase], halo_left.at[phase], halo_right.at[phase],
-        corner.at[phase, 0], corner.at[phase, 1], corner.at[phase, 2], corner.at[phase, 3],
-    ]
+    def landing(phase):
+        reach = PR if phase == PIL else RMAX
+        far, near = pl.ds(RMAX - reach, reach), pl.ds(0, reach)
+        return [
+            halo_top.at[phase, far], halo_bottom.at[phase, near],
+            halo_left.at[phase], halo_right.at[phase],
+            corner.at[phase, 0, far], corner.at[phase, 1, far],
+            corner.at[phase, 2, near], corner.at[phase, 3, near],
+        ]
+
+    half = tr // 2
+    lower = lax.broadcasted_iota(jnp.int32, (half, B), 1) < RMAX
+
+    def pack(phase):
+        a = padded[phase, 0:half, 0:B]
+        b = padded[phase, half:tr, 0:B]
+        packed[phase, 0] = jnp.where(lower, pltpu.roll(b, RMAX, axis=1), a)
+        a = padded[phase, 0:half, last : last + B]
+        b = padded[phase, half:tr, last : last + B]
+        packed[phase, 1] = jnp.where(lower, a, pltpu.roll(b, RMAX, axis=1))
 
     def send(phase):
+        pack(phase)
         for n in range(8):
             dr, dc = steps[n]
 
@@ -162,8 +182,6 @@
                 piece = x[a : a + 8, b : b + 128]
                 total = piece if total is None else total + piece
         return total
-
-    CLS, PIL, ONE, TWO = 0, 1, 2, 3
 
     def prepare(i, total):
         at = pl.ds(pl.multiple_of(i * CHUNK, CHUNK), CHUNK)
@@ -187,6 +205,11 @@
     send(CLS)
     for phase in range(4):
         clear(phase)
+    if PR < RMAX:
+        halo_top[PIL, 0 : RMAX - PR, :] = jnp.zeros((RMAX - PR, wide), F32)
+        halo_bottom[PIL, PR:RMAX, :] = jnp.zeros((RMAX - PR, wide), F32)
+        corner[PIL, 0:2, 0 : RMAX - PR, :] = jnp.zeros((2, RMAX - PR, B), F32)
+        corner[PIL, 2:4, PR:RMAX, :] = jnp.zeros((2, RMAX - PR, B), F32)
 
     for n in range(classes_n + 1):
         radius = F32(PR) if n == classes_n else radius_ref[n].astype(F32)
@@ -231,14 +254,24 @@
 
         lax.fori_loop(0, RMAX // CHUNK, step, 0)
 
+        low_lanes = lax.broadcasted_iota(jnp.int32, (CHUNK, B), 1) < RMAX
+
         def middle(i, _):
             at = pl.ds(pl.multiple_of(i * CHUNK, CHUNK), CHUNK)
+            under = pl.ds(pl.multiple_of(i * CHUNK + half, CHUNK), CHUNK)
             inner = pl.ds(pl.multiple_of(i * CHUNK + RMAX, CHUNK), CHUNK)
-            put(inner, left, padded[phase, at, left] + halo_left[phase, at, :], masks)
-            put(inner, right, padded[phase, at, right] + halo_right[phase, at, :], masks)
-            return 0
-
-        lax.fori_loop(0, chunks, middle, 0)
+            inner_under = pl.ds(pl.multiple_of(i * CHUNK + half + RMAX, CHUNK), CHUNK)
+            x = halo_left[phase, at, :]
+            turned = pltpu.roll(x, RMAX, axis=1)
+            put(inner, left, jnp.where(low_lanes, x, padded[phase, at, left]), masks)
+            put(inner_under, left, jnp.where(low_lanes, turned, padded[phase, under, left]), masks)
+            x = halo_right[phase, at, :]
+            turned = pltpu.roll(x, RMAX, axis=1)
+            put(inner, right, jnp.where(low_lanes, padded[phase, at, right], x), masks)
+            put(inner_under, right, jnp.where(low_lanes, padded[phase, under, right], turned), masks)
+            return 0
+
+        lax.fori_loop(0, half // CHUNK, middle, 0)
 
     def row_piece(i, places, labelled):
         source = pl.ds(pl.multiple_of(i * B, B), K)
@@ -371,11 +404,6 @@
         send(phase)
         return total
 
-    sweep(PIL, False)
-    col_sweep(field, False)
-    log_total = adapt(ONE, lambda at: field[at, :])
-    reduce_start(0, log_total)
-
     def own_masks(i, _):
         at = pl.ds(pl.multiple_of(i * CHUNK, CHUNK), CHUNK)
         inner = pl.ds(pl.multiple_of(i * CHUNK + RMAX, CHUNK), CHUNK)
@@ -383,32 +411,29 @@
         return 0
 
     lax.fori_loop(0, chunks, own_masks, 0)
+    sweep(PIL, False)
+    col_sweep(field, False)
+    log_total = adapt(ONE, lambda at: field[at, :])
+    reduce_start(0, log_total)
+
     arrived(CLS, range(8))
     rows_in(CLS, True)
     cols_in(CLS, True)
 
-    sweep(ONE, True, [lambda: reduce_middle(0)])
-    col_sweep(field, True)
+    sweep(ONE, True, [lambda: None, lambda: reduce_middle(0)])
+    col_sweep(first_ref, True)
     inverse = reduce_end(0)
+    inverse_ref[0:8, :] = jnp.broadcast_to(inverse, (8, 128))
 
     def first_density(at):
-        density = field[at, :] * inverse
-        first_ref[at, :] = density
-        return density
+        return first_ref[at, :] * inverse
 
     log_total = adapt(TWO, first_density)
     reduce_start(1, log_total)
 
-    sweep(TWO, True, [lambda: reduce_middle(1)])
-    col_sweep(field, True)
-    inverse_two = reduce_end(1)
-
-    def finish(i, _):
-        at = pl.ds(pl.multiple_of(i * CHUNK, CHUNK), CHUNK)
-        second_ref[at, :] = field[at, :] * inverse_two
-        return 0
-
-    lax.fori_loop(0, chunks, finish, 0)
+    sweep(TWO, True, [lambda: None, lambda: reduce_middle(1)])
+    col_sweep(second_ref, True)
+    inverse_ref[8:16, :] = jnp.broadcast_to(reduce_end(1), (8, 128))
     for phase in range(4):
         sent(phase)
 
@@ -419,15 +444,16 @@
     wide, tall = tc + 2 * RMAX, tr + 2 * RMAX
     vmem = pl.BlockSpec(memory_space=pltpu.VMEM)
     out = jax.ShapeDtypeStruct((tr, tc), F32)
-    return pl.pallas_call(
+    first, second, inverse = pl.pallas_call(
         functools.partial(kernel, rows, cols, n),
-        out_shape=(out, out),
+        out_shape=(out, out, jax.ShapeDtypeStruct((16, 128), F32)),
         in_specs=[pl.BlockSpec(memory_space=pltpu.SMEM), vmem, vmem, vmem],
-        out_specs=(vmem, vmem),
+        out_specs=(vmem, vmem, vmem),
         scratch_shapes=[
             pltpu.VMEM((tr, tc), F32),
             pltpu.VMEM((tr, tc), F32),
             pltpu.VMEM((4, tr, wide), F32),
+            pltpu.VMEM((4, 2, tr // 2, B), F32),
             pltpu.VMEM((tall, wide), BF16),
             pltpu.VMEM((tall, wide), BF16),
             pltpu.VMEM((n, tall, wide), BF16),
@@ -437,8 +463,8 @@
             pltpu.VMEM((n + 1, 2 * K, 2 * B), BF16),
             pltpu.VMEM((4, RMAX, wide), F32),
             pltpu.VMEM((4, RMAX, wide), F32),
-            pltpu.VMEM((4, tr, B), F32),
-            pltpu.VMEM((4, tr, B), F32),
+            pltpu.VMEM((4, tr // 2, B), F32),
+            pltpu.VMEM((4, tr // 2, B), F32),
             pltpu.VMEM((4, 4, RMAX, B), F32),
             pltpu.VMEM((2, 2, 16, 128), F32),
             pltpu.VMEM((2, rows, 16, 128), F32),
@@ -454,6 +480,7 @@
             collective_id=0, has_side_effects=True, vmem_limit_bytes=60 * 2**20
         ),
     )(class_radius, counts, sample_weights, classes)
+    return first * inverse[0, 0], second * inverse[8, 0]
 
 
 def solution(mesh):

time: 81.3 us -> 72.8 us (0.90)
  Pallas kernels: 75.3 us -> 64.4 us
  other arithmetic: 0 us -> 6.3 us
  local copies, waits for them, and re-layouts: 4.63 us -> 1.27 us
    pallas_call x1, Pallas kernels: 75.3 us -> 64.4 us  [body(): pl.pallas_call(functools.partial(kernel, rows, cols, n), out_shape=(out,...]
    mul x0 -> x1, other arithmetic: none -> 6.3 us  [body(): return (first * inverse[0, 0], second * inverse[8, 0])]
    unnamed x4 -> x0, local copies, waits for them, and re-layouts: 4.63 us -> none
    slice x0 -> x1, local copies, waits for them, and re-layouts: none -> 1.27 us  [body(): return (first * inverse[0, 0], second * inverse[8, 0])]
where the time goes in v2:
time: 72.8 us; the launch traced here: 72.6 us
  Pallas kernels  64.4 us (88%)
  other arithmetic  6.3 us (9%)
  local copies, waits for them, and re-layouts  1.27 us (2%)
    pallas_call x1, Pallas kernels, body(): pl.pallas_call(functools.partial(kernel, rows, cols, n), out_shape=(out,...  64.4 us
    mul x1, other arithmetic, body(): return (first * inverse[0, 0], second * inverse[8, 0])  6.3 us

profile of v2, /device:TPU:12, one launch (start us, length us, event | category | flops | bytes accessed | tf_op | source)
XLA Modules:
  0.0 72.6 jit_solution(3942590922775084841)
XLA Ops:
  0.6 64.4 %shard_map.59 = (f32[512,1024]{1,0:T(8,128)}, f32[512,1024]{1,0:T(8,128)}, f32[16,128]{1,0:T(8,128)}) custom-call(s32[4]{0:T(128)} %radius_ref.1, s32[512,1024]{1,0:T(8,128)} %counts_ref.1, f32[512,1024]{1,0:T(8,128)} %weights_ref.1, s32[512,1024]{1,0:T(8,128)} %classes_ref.1), custom_call_target="tpu_custom_call" | custom-call | tf_op jit(solution)/shard_map/pallas_call | solution.py:447
  65.0 1.3 %fusion = (f32[1,1]{1,0:T(1,128)}, f32[1,1]{1,0:T(1,128)}) fusion(f32[16,128]{1,0:T(8,128)} %get-tuple-element.6), kind=kLoop, calls=%fused_computation.2 | loop fusion | bytes 16 | tf_op jit(solution)/shard_map/slice | solution.py:483
  66.3 6.3 %broadcast_multiply_fusion = (f32[512,1024]{1,0:T(8,128)}, f32[512,1024]{1,0:T(8,128)}) fusion(f32[512,1024]{1,0:T(8,128)} %get-tuple-element.7, f32[]{:T(128)} %bitcast.1, f32[512,1024]{1,0:T(8,128)} %get-tuple-element.5, f32[]{:T(128)} %bitcast), kind=kLoop, calls=%fused_computation | loop fusion | flops 1048576 | bytes 8388616 | tf_op jit(solution)/shard_map/mul | solution.py:483
